TPU v7x, 1024 devices: a whole 4x8x16 slice. The times are simulated.
1024 devices in a mesh: dp: 8 (over z_lo), mx: 16 (over y, z_hi), my: 8 (over x, core).
Axes of the slice: x: 4, y: 8, z: 16 (z_hi: 2, z_lo: 8; z = z_hi * 8 + z_lo), core: 2. Of those that a mesh axis runs over, the one named last changes fastest.
Arguments:
- tokens: bfloat16 [2048, 6144], P(('dp', 'mx')), may hold values from -6 to 6
- w_in: bfloat16 [6144, 24576], P('my', 'mx'), may hold values from -0.078125 to 0.078125
- w_out: bfloat16 [16384, 6144], P('mx', 'my'), may hold values from -0.046875 to 0.046875
- cotangent: bfloat16 [2048, 6144], P(('dp', 'mx'), 'my'), may hold values from -0.29882812 to 0.29882812
Outputs:
- grad_in: bfloat16 [8, 768, 24576], P('dp', 'my', 'mx')
- grad_out: bfloat16 [8, 2048, 6144], P('dp', 'mx', 'my')
All inputs are finite; a program needn't handle non-finite values.
Results may differ from a plain program's by a relative error of at most 0.03.
Values may be sent and summed in bfloat16 or wider, within the bound.
No kernel may reach another device: no remote copies, remote signals or barrier semaphores. Data moves between devices by JAX's collectives and lax.ppermute only.
A program may use at most 32 MiB of HBM per device.

v0:
```python
import jax
import jax.numpy as jnp
from jax import lax
from jax.experimental import pallas as pl
from jax.experimental.pallas import tpu as pltpu
from jax.sharding import Mesh
from jax.sharding import PartitionSpec as P

HEAD = 128
HEADS_DEV = 2
PATCHES = 128
IMAGES = 2
UNITS = 384
EPS = 1e-06

INTERPRET = False
VMEM_LIMIT = 48 * 2**20

DP = ("dh", "dl")
MX = ("y", "zh")
MY = ("x", "c")

F32 = jnp.float32
BF16 = jnp.bfloat16


def stay(values):
    return pltpu.with_memory_space_constraint(values, pltpu.HBM)


def params():
    return pltpu.CompilerParams(vmem_limit_bytes=VMEM_LIMIT)


def norm_kernel(place_ref, tokens_ref, mine_ref, cot_ref, out_ref):
    x = tokens_ref[...].astype(F32)
    mean = jnp.mean(x, axis=-1, keepdims=True)
    center = x - mean
    spread = jnp.mean(center * center, axis=-1, keepdims=True)
    mine = (mine_ref[...].astype(F32) - mean) * lax.rsqrt(spread + EPS)
    out_ref[0] = mine.astype(BF16)
    out_ref[1] = cot_ref[...]


def norm_rows(place, tokens, cotangent):
    rows, features = tokens.shape
    dblock = cotangent.shape[1]
    return pl.pallas_call(
        norm_kernel,
        out_shape=jax.ShapeDtypeStruct((2, rows, dblock), BF16),
        grid_spec=pltpu.PrefetchScalarGridSpec(
            num_scalar_prefetch=1,
            grid=(1,),
            in_specs=[
                pl.BlockSpec((rows, features), lambda s, place: (0, 0)),
                pl.BlockSpec((rows, dblock), lambda s, place: (0, place[0])),
                pl.BlockSpec((rows, dblock), lambda s, place: (0, 0)),
            ],
            out_specs=pl.BlockSpec((2, rows, dblock), lambda s, place: (0, 0, 0)),
        ),
        compiler_params=params(),
        interpret=INTERPRET,
    )(place, stay(tokens), stay(tokens), stay(cotangent))


def longer_kernel(rows_ref, out_ref):
    sides, kinds, count, _ = rows_ref.shape
    for third, kind in enumerate((1, 0, 1)):
        for side in range(sides):
            first = (third * sides + side) * count
            out_ref[first : first + count] = rows_ref[side, kind]


def longer_rows(rows):
    sides, _, count, dblock = rows.shape
    shape = (3 * sides * count, dblock)
    return pl.pallas_call(
        longer_kernel,
        out_shape=jax.ShapeDtypeStruct(shape, BF16),
        grid=(1,),
        in_specs=[pl.BlockSpec(rows.shape, lambda s: (0, 0, 0, 0))],
        out_specs=pl.BlockSpec(shape, lambda s: (0, 0)),
        compiler_params=params(),
        interpret=INTERPRET,
    )(rows)


def products_kernel(y_ref, cot_ref, w_ref, va, vb, vc, out_ref, flag_ref):
    total = IMAGES * PATCHES
    dblock = w_ref.shape[0]
    y = y_ref[...].reshape(total, dblock)
    cot = cot_ref[...].reshape(total, dblock)
    pre = jnp.dot(y, w_ref[...], preferred_element_type=F32).astype(BF16)
    flag_ref[...] = jnp.zeros_like(flag_ref)

    def back(v):
        terms = lax.dot_general(cot, v, (((1,), (1,)), ((), ())), preferred_element_type=F32)
        return terms.astype(BF16)

    def put(s, first, values):
        width = values.shape[1]
        out_ref[0, :, s, :, first : first + width] = values.reshape(IMAGES, PATCHES, width)

    @pl.when(pl.program_id(0) == 0)
    def heads():
        grad = back(va[...])
        for s in range(2):
            for a in range(3):
                first = (2 * a + s) * HEAD
                put(s, a * HEAD, pre[:, first : first + HEAD])
            put(s, UNITS, grad[:, s * HEAD : (s + 1) * HEAD])
            put(s, UNITS + HEAD, jnp.zeros((total, 2 * HEAD), BF16))

    @pl.when(pl.program_id(0) == 1)
    def units():
        grad = back(jnp.concatenate([va[...], vb[...], vc[...]], axis=0))
        for s in range(2):
            put(s, 0, pre[:, s * UNITS : (s + 1) * UNITS])
            put(s, UNITS, grad[:, s * UNITS : (s + 1) * UNITS])


def products(gathered, w_in, w_out):
    lines, sides, _, rows, dblock = gathered.shape

    def kind(which):
        return pl.BlockSpec(
            (lines, sides, pl.squeezed, rows, dblock), lambda s: (0, 0, which, 0, 0)
        )

    def v_rows(block):
        return pl.BlockSpec((2 * HEAD, dblock), lambda s: (block(s), 0))

    return pl.pallas_call(
        products_kernel,
        out_shape=(
            pltpu.HBM((2, IMAGES, 2, PATCHES, 2 * UNITS), BF16),
            pltpu.HBM((8, HEAD), F32),
        ),
        grid=(2,),
        in_specs=[
            kind(0),
            kind(1),
            pl.BlockSpec((dblock, 2 * UNITS), lambda s: (0, s)),
            v_rows(lambda s: s),
            v_rows(lambda s: 2),
            v_rows(lambda s: 3),
        ],
        out_specs=[
            pl.BlockSpec((1, IMAGES, 2, PATCHES, 2 * UNITS), lambda s: (s, 0, 0, 0, 0)),
            pl.BlockSpec((8, HEAD), lambda s: (0, 0)),
        ],
        compiler_params=params(),
        interpret=INTERPRET,
    )(gathered, gathered, stay(w_in), *[stay(w_out)] * 3)


def exact(a, b, contract):
    return lax.dot_general(
        a, b, (contract, ((), ())), precision=lax.Precision.HIGHEST, preferred_element_type=F32
    )


def head_norm(values):
    center = values - jnp.mean(values, axis=-1, keepdims=True)
    scale = lax.rsqrt(jnp.mean(center * center, axis=-1, keepdims=True) + EPS)
    return center * scale, scale


def head_norm_pull(normed, scale, grad):
    along = jnp.mean(grad * normed, axis=-1, keepdims=True)
    return scale * (grad - jnp.mean(grad, axis=-1, keepdims=True) - normed * along)


def unit_kernel(place_ref, terms_ref, earlier_ref, hidden_ref, d_pre_ref):
    summed = terms_ref[0].astype(F32)
    for part in range(1, terms_ref.shape[0]):
        summed = summed + terms_ref[part].astype(F32)
    pre = summed[:, :UNITS].astype(BF16).astype(F32)
    grad = summed[:, UNITS:]

    @pl.when(place_ref[0] < 4)
    def attention():
        value = pre[:, 2 * HEAD :]
        d_out = grad[:, :HEAD]
        query, query_scale = head_norm(pre[:, :HEAD])
        key, key_scale = head_norm(pre[:, HEAD : 2 * HEAD])
        weights = jnp.exp(exact(query, key, ((1,), (1,))) * HEAD ** (-0.5))
        weights = weights / jnp.sum(weights, axis=-1, keepdims=True)
        out = exact(weights, value, ((1,), (0,)))
        d_value = exact(weights, d_out, ((0,), (0,)))
        d_weights = exact(d_out, value, ((1,), (1,)))
        along = jnp.sum(d_weights * weights, axis=-1, keepdims=True)
        d_scores = weights * (d_weights - along) * HEAD ** (-0.5)
        d_query = exact(d_scores, key, ((1,), (0,)))
        d_key = exact(d_scores, query, ((0,), (0,)))
        for i in range(IMAGES):
            hidden_ref[i, :, :HEAD] = out.astype(BF16)
            hidden_ref[i, :, HEAD:] = jnp.zeros((PATCHES, 2 * HEAD), BF16)
        d_pre_ref[:, :HEAD] = head_norm_pull(query, query_scale, d_query).astype(BF16)
        d_pre_ref[:, HEAD : 2 * HEAD] = head_norm_pull(key, key_scale, d_key).astype(BF16)
        d_pre_ref[:, 2 * HEAD :] = d_value.astype(BF16)

    @pl.when(place_ref[0] >= 4)
    def units():
        below = 0.5 * (1.0 + lax.erf(pre * 2.0**-0.5))
        density = jnp.exp(-0.5 * pre * pre) * 0.3989422804014327
        for i in range(IMAGES):
            hidden_ref[i] = (pre * below).astype(BF16)
        d_pre_ref[...] = (grad * (below + pre * density)).astype(BF16)


def unit(place, terms, earlier):
    return pl.pallas_call(
        unit_kernel,
        out_shape=(
            jax.ShapeDtypeStruct((IMAGES, PATCHES, UNITS), BF16),
            jax.ShapeDtypeStruct((PATCHES, UNITS), BF16),
        ),
        grid_spec=pltpu.PrefetchScalarGridSpec(
            num_scalar_prefetch=1,
            grid=(1,),
            in_specs=[
                pl.BlockSpec(terms.shape, lambda s, place: (0, 0, 0)),
                pl.BlockSpec(memory_space=pl.ANY),
            ],
            out_specs=[
                pl.BlockSpec((IMAGES, PATCHES, UNITS), lambda s, place: (0, 0, 0)),
                pl.BlockSpec((PATCHES, UNITS), lambda s, place: (0, 0)),
            ],
        ),
        compiler_params=params(),
        interpret=INTERPRET,
    )(place, terms, earlier)


def by_owner_kernel(place_ref, pieces_ref, earlier_ref, out_ref):
    for s in range(2):
        out_ref[s] = pieces_ref[0, 0, s, :, :HEAD]
        for a in range(3):
            out_ref[2 + 3 * s + a] = pieces_ref[1, 0, s, :, a * HEAD : (a + 1) * HEAD]


def by_owner(place, pieces, earlier):
    rows = pieces.shape[-2]
    return pl.pallas_call(
        by_owner_kernel,
        out_shape=jax.ShapeDtypeStruct((8, rows, HEAD), BF16),
        grid_spec=pltpu.PrefetchScalarGridSpec(
            num_scalar_prefetch=1,
            grid=(1,),
            in_specs=[
                pl.BlockSpec(
                    (2, 1, 2, rows, UNITS), lambda s, place: (0, place[0] // 4, 0, 0, 0)
                ),
                pl.BlockSpec(memory_space=pl.ANY),
            ],
            out_specs=pl.BlockSpec((8, rows, HEAD), lambda s, place: (0, 0, 0)),
        ),
        compiler_params=params(),
        interpret=INTERPRET,
    )(place, pieces, earlier)


def halves_kernel(side_ref, keep_in, give_in, earlier_ref, keep_ref, give_ref):
    for given, ref in ((keep_in, keep_ref), (give_in, give_ref)):
        ref[...] = given[...].reshape(ref.shape[1], ref.shape[0]).T


def halves(side, gathered, earlier):
    lines, sides, _, rows, dblock = gathered.shape
    half = dblock // 2
    block = (lines, sides, pl.squeezed, rows, half)
    turned = (half, lines * sides * rows)
    shape = jax.ShapeDtypeStruct(turned, BF16)
    return pl.pallas_call(
        halves_kernel,
        out_shape=(shape, shape),
        grid_spec=pltpu.PrefetchScalarGridSpec(
            num_scalar_prefetch=1,
            grid=(1,),
            in_specs=[
                pl.BlockSpec(block, lambda s, side: (0, 0, 0, 0, side[0])),
                pl.BlockSpec(block, lambda s, side: (0, 0, 0, 0, 1 - side[0])),
                pl.BlockSpec(memory_space=pl.ANY),
            ],
            out_specs=[pl.BlockSpec(turned, lambda s, side: (0, 0))] * 2,
        ),
        compiler_params=params(),
        interpret=INTERPRET,
    )(side, gathered, gathered, stay(earlier))


def cotangent_kernel(rows_ref, *refs):
    refs[-1][...] = rows_ref[...]


def cotangent_rows(gathered, count, earlier):
    groups, _, dblock = gathered.shape
    part = pl.BlockSpec((groups, count, dblock), lambda s: (0, 0, 0))
    return pl.pallas_call(
        cotangent_kernel,
        out_shape=pltpu.HBM((groups, count, dblock), BF16),
        grid=(1,),
        in_specs=[part] + [pl.BlockSpec(memory_space=pl.ANY)] * len(earlier),
        out_specs=part,
        compiler_params=params(),
        interpret=INTERPRET,
    )(stay(gathered), *earlier)


def grad_out_kernel(hidden_ref, cot_ref, out_ref, flag_ref, sum_ref):
    step = pl.program_id(0)
    total = cot_ref.shape[0] * cot_ref.shape[1] * cot_ref.shape[2]
    hidden = hidden_ref[...].reshape(total, HEAD)
    cot = cot_ref[...].reshape(total, cot_ref.shape[-1])
    terms = lax.dot_general(hidden, cot, (((0,), (0,)), ((), ())), preferred_element_type=F32)

    @pl.when(step == 0)
    def first():
        sum_ref[...] = terms

    @pl.when(step > 0)
    def later():
        sum_ref[...] += terms

    @pl.when(step == pl.num_programs(0) - 1)
    def last():
        out_ref[...] = sum_ref[...].astype(BF16)
        flag_ref[...] = jnp.zeros_like(flag_ref)


def grad_out_rows(hidden, cot):
    lines, groups, rows, dblock = cot.shape
    steps = 2
    return pl.pallas_call(
        grad_out_kernel,
        out_shape=(
            jax.ShapeDtypeStruct((HEAD, dblock), BF16),
            pltpu.HBM((8, HEAD), F32),
        ),
        grid=(steps,),
        in_specs=[
            pl.BlockSpec((lines // steps, groups, rows, HEAD), lambda s: (s, 0, 0, 0)),
            pl.BlockSpec((lines // steps, groups, rows, dblock), lambda s: (s, 0, 0, 0)),
        ],
        out_specs=[
            pl.BlockSpec((HEAD, dblock), lambda s: (0, 0)),
            pl.BlockSpec((8, HEAD), lambda s: (0, 0)),
        ],
        scratch_shapes=[pltpu.VMEM((HEAD, dblock), F32)],
        compiler_params=params(),
        interpret=INTERPRET,
    )(hidden, stay(cot))


def grad_in_kernel(y_own_ref, y_other_ref, own_ref, other_ref, out_ref):
    for t in range(2):
        terms = 0.0
        for y_ref, ref in ((y_own_ref, own_ref), (y_other_ref, other_ref)):
            rows = [
                jnp.concatenate([ref[4 * t + 2 * i + s] for s in range(2)], axis=1)
                for i in range(IMAGES)
            ]
            d_pre = jnp.concatenate(rows, axis=0)
            terms = terms + jnp.dot(y_ref[...], d_pre, preferred_element_type=F32)
        terms = terms.astype(BF16)
        if t == 0:
            for s in range(2):
                for a in range(3):
                    first, from_ = (2 * a + s) * HEAD, (3 * s + a) * HEAD
                    out_ref[:, first : first + HEAD] = terms[:, from_ : from_ + HEAD]
        else:
            out_ref[:, 2 * UNITS :] = terms


def grad_in_terms(y_own, y_other, own, other):
    features = y_own.shape[0]
    width = 4 * UNITS
    y = pl.BlockSpec(y_own.shape, lambda s: (0, 0))
    whole = pl.BlockSpec(own.shape, lambda s: (0, 0, 0))
    return pl.pallas_call(
        grad_in_kernel,
        out_shape=pltpu.HBM((features, width), BF16),
        grid=(1,),
        in_specs=[y, y, whole, whole],
        out_specs=pl.BlockSpec((features, width), lambda s: (0, 0)),
        compiler_params=params(),
        interpret=INTERPRET,
    )(y_own, y_other, own, other)


def sum_kernel(parts_ref, earlier_ref, out_ref):
    summed = parts_ref[0].astype(F32)
    for part in range(1, parts_ref.shape[0]):
        summed = summed + parts_ref[part].astype(F32)
    out_ref[...] = summed.astype(BF16)


def sum_parts(parts, earlier):
    shape = parts.shape[1:]
    return pl.pallas_call(
        sum_kernel,
        out_shape=jax.ShapeDtypeStruct(shape, BF16),
        grid=(1,),
        in_specs=[
            pl.BlockSpec(parts.shape, lambda s: (0, 0, 0)),
            pl.BlockSpec(memory_space=pl.ANY),
        ],
        out_specs=pl.BlockSpec(shape, lambda s: (0, 0)),
        compiler_params=params(),
        interpret=INTERPRET,
    )(parts, stay(earlier))


def swap(values, axis):
    return lax.ppermute(values, axis, [(0, 1), (1, 0)])


def send(values, axis):
    shape = values.shape
    flat = values.reshape((shape[0] * shape[1],) + shape[2:])
    return lax.all_to_all(flat, axis, 0, 0, tiled=True).reshape(shape)


def shards(tokens, w_in, w_out, cotangent):
    parts = lax.axis_size(MY)
    groups = lax.axis_size(DP)
    place = lax.axis_index(MY).astype(jnp.int32).reshape(1)
    side = lax.axis_index("dh").astype(jnp.int32).reshape(1)
    dblock = w_in.shape[0]
    total = IMAGES * PATCHES
    kinds = (2, IMAGES, 2)
    lines = 8
    block = total // lines

    with jax.named_scope("token_rows"):
        mine = norm_rows(place, tokens, cotangent)
        rows = lax.all_gather(mine, "zh", axis=0, tiled=False)
        longer = longer_rows(rows)
        gathered = lax.all_gather(rows, "y", axis=0, tiled=False)

    with jax.named_scope("units"):
        partial, flag = products(gathered, w_in, w_out)
        terms = send(partial.reshape(parts, PATCHES, 2 * UNITS), MY)

    with jax.named_scope("y_of_two_groups"):
        y_own, y_give = halves(side, gathered, flag)
        y_other = swap(y_give, "dh")

    with jax.named_scope("units"):
        hidden, d_pre = unit(place, terms, y_own)

    with jax.named_scope("d_pre_of_two_groups"):
        d_pre_other = swap(d_pre, "dh")
        own = lax.all_gather(d_pre, MY, axis=0, tiled=False)
        other = lax.all_gather(d_pre_other, MY, axis=0, tiled=False)
        grad_in = grad_in_terms(y_own, y_other, own, other)
        grad_in = send(grad_in.reshape(4, dblock // 8, grad_in.shape[1]), "dl")

    with jax.named_scope("hidden_of_all_groups"):
        pieces = send(hidden.reshape(parts, block, UNITS), MY)
        owned = by_owner(place, pieces.reshape(kinds + (block, UNITS)), own)

    with jax.named_scope("cotangent_of_all_groups"):
        count = rows.shape[0] * rows.shape[2]
        cot_rows = lax.all_gather(longer, DP, axis=0, tiled=False)
        cot_rows = cotangent_rows(cot_rows, count, (owned, d_pre_other, y_other))
        cot_all = lax.all_gather(cot_rows, "y", axis=0, tiled=False)
        held = cot_all.shape[0]
        cot_all = cot_all.reshape(held, groups, lines // held, block, dblock)
        cot_all = cot_all.swapaxes(1, 2).reshape(lines, groups, block, dblock)

    with jax.named_scope("hidden_of_all_groups"):
        owned = lax.all_gather(send(owned, DP), MY, axis=0, tiled=False)
        grad_out, done = grad_out_rows(owned, cot_all)

    with jax.named_scope("grad_in_sum"):
        grad_in = sum_parts(grad_in, done)

    return grad_in[None], grad_out[None]


def solution(mesh):
    sizes = dict(mesh.shape)
    lines = sizes["mx"] // 2
    cut = (2, sizes["dp"] // 2, lines, 2, sizes["my"] // 2, 2)
    fine = Mesh(mesh.devices.reshape(cut), DP + MX + MY)
    return jax.shard_map(
        shards,
        mesh=fine,
        in_specs=(P(DP + MX, None), P(MY, MX), P(MX, MY), P(DP + MX, MY)),
        out_specs=(P(DP, MY, MX), P(DP, MX, MY)),
        check_vma=False,
    )
```

profile of v0, /device:TPU:1, one launch (start us, length us, event | category | flops | bytes accessed | tf_op | source)
XLA Modules:
  0.0 181.5 jit_solution(15403483219512985586)
XLA Ops:
  7.2 0.0 all-gather.10.cloned.1.call-start
  7.2 1.3 token_rows.2
  8.5 20.3 %all-gather = bf16[4,16,768]{2,1,0:T(8,128)(2,1)S(1)} all-gather(bf16[2,16,768]{2,1,0:T(8,128)(2,1)S(1)} %token_rows.2), channel_id=2, replica_groups=mesh['dh'=2,'dl'=4,'y'=8,'zh'=2,'x'=4,'c'=2] {'zh'}, dimensions={0}, use_global_device_ids=true | all-gather | bytes 147456 | tf_op jit(solution)/shard_map/token_rows/all_gather | solution.py:438
  28.8 0.7 token_rows.3
  29.5 22.1 %all-gather.1 = bf16[16,2,16,768]{3,2,1,0:T(8,128)(2,1)S(1)} all-gather(bf16[2,2,16,768]{3,2,1,0:T(8,128)(2,1)S(1)} %bitcast.24), channel_id=3, replica_groups=mesh['dh'=2,'dl'=4,'y'=8,'zh'=2,'x'=4,'c'=2] {'y'}, dimensions={0}, use_global_device_ids=true | all-gather | bytes 884736 | tf_op jit(solution)/shard_map/token_rows/all_gather | solution.py:440
  51.6 4.4 %units.2 = (bf16[2,2,2,128,768]{4,3,2,1,0:T(8,128)(2,1)}, f32[8,128]{1,0:T(8,128)}) custom-call(bf16[8,2,2,16,768]{4,3,2,1,0:T(8,128)(2,1)S(1)} %bitcast.15, bf16[8,2,2,16,768]{4,3,2,1,0:T(8,128)(2,1)S(1)} %bitcast.16, bf16[768,1536]{1,0:T(8,128)(2,1)} %w_ref.1, bf16[1024,768]{1,0:T(8,128)(2,1)} %vc.1, bf16[1024,768]{1,0:T(8,128)(2,1)} %vc.1, ...), custom_call_target="tpu_custom_call" | custom-call | tf_op jit(solution)/shard_map/units/pallas_call | solution.py:133
  56.0 14.7 %all-to-all-start = ((bf16[8,128,768]{2,1,0:T(8,128)(2,1)}), bf16[8,128,768]{2,1,0:T(8,128)(2,1)S(1)}, u32[]{:S(2)}, u32[]{:S(2)}) async-start(bf16[8,128,768]{2,1,0:T(8,128)(2,1)} %bitcast.28), calls=%async_computation | async-start | bytes 3145728 | tf_op jit(solution)/shard_map/units/all_to_all | solution.py:422
  70.8 0.2 y_of_two_groups.1
  70.9 4.4 %collective-permute-start = (bf16[384,256]{1,0:T(8,128)(2,1)S(1)}, bf16[384,256]{1,0:T(8,128)(2,1)S(1)}, u32[]{:S(2)}, u32[]{:S(2)}) collective-permute-start(bf16[384,256]{1,0:T(8,128)(2,1)S(1)} %get-tuple-element.12), channel_id=1, source_target_pairs={{0,512},{512,0},{1,513},{513,1},{2,514},{514,2},{3,515},{515,3},{4... | collective-permute-start | bytes 589832 | tf_op jit(solution)/shard_map/y_of_two_groups/ppermute | solution.py:416
  75.4 16.3 %all-to-all-done.terms_ref = bf16[8,128,768]{2,1,0:T(8,128)(2,1)S(1)} async-done(((bf16[8,128,768]{2,1,0:T(8,128)(2,1)}), bf16[8,128,768]{2,1,0:T(8,128)(2,1)S(1)}, u32[]{:S(2)}, u32[]{:S(2)}) %all-to-all-start) | async-done | bytes 1572896 | tf_op jit(solution)/shard_map/units/all_to_all | solution.py:422
  91.6 2.3 %units.3 = (bf16[2,128,384]{2,1,0:T(8,128)(2,1)}, bf16[128,384]{1,0:T(8,128)(2,1)S(1)}) custom-call(s32[1]{0:T(128)} %bitcast.1.place_ref, bf16[8,128,768]{2,1,0:T(8,128)(2,1)S(1)} %all-to-all-done.terms_ref, bf16[384,256]{1,0:T(8,128)(2,1)S(1)} %get-tuple-element.11.earlier_ref.y_own_ref), custom_call_target="tpu_custom_call" | custom-call | tf_op jit(solution)/shard_map/units/pallas_call | solution.py:213
  93.9 4.1 %all-to-all-start.2 = ((bf16[8,32,384]{2,1,0:T(8,128)(2,1)}), bf16[8,32,384]{2,1,0:T(8,128)(2,1)S(1)}, u32[]{:S(2)}, u32[]{:S(2)}) async-start(bf16[8,32,384]{2,1,0:T(8,128)(2,1)} %bitcast.8), calls=%async_computation.2 | async-start | bytes 393216 | tf_op jit(solution)/shard_map/hidden_of_all_groups/all_to_all | solution.py:422
  97.9 4.4 %collective-permute-start.1 = (bf16[128,384]{1,0:T(8,128)(2,1)S(1)}, bf16[128,384]{1,0:T(8,128)(2,1)S(1)}, u32[]{:S(2)}, u32[]{:S(2)}) collective-permute-start(bf16[128,384]{1,0:T(8,128)(2,1)S(1)} %get-tuple-element.14), channel_id=1, source_target_pairs={{0,512},{512,0},{1,513},{513,1},{2,514},{514,2},{3,515},{515,3},{4... | collective-permute-start | bytes 294920 | tf_op jit(solution)/shard_map/d_pre_of_two_groups/ppermute | solution.py:416
  102.3 14.4 %all-gather.2 = bf16[1024,384]{1,0:T(8,128)(2,1)S(1)} all-gather(bf16[128,384]{1,0:T(8,128)(2,1)S(1)} %get-tuple-element.14), channel_id=4, replica_groups=mesh['dh'=2,'dl'=4,'y'=8,'zh'=2,'x'=4,'c'=2] {'x','c'}, dimensions={0}, use_global_device_ids=true | all-gather | bytes 884736 | tf_op jit(solution)/shard_map/d_pre_of_two_groups/all_gather | solution.py:455
  116.7 0.6 hidden_of_all_groups.2.refs_0_
  117.4 1.8 cotangent_of_all_groups.1
  119.2 4.3 %all-to-all-start.3 = ((bf16[8,32,128]{2,1,0:T(8,128)(2,1)}), bf16[8,32,128]{2,1,0:T(8,128)(2,1)S(1)}, u32[]{:S(2)}, u32[]{:S(2)}) async-start(bf16[8,32,128]{2,1,0:T(8,128)(2,1)} %hidden_of_all_groups.2.refs_0_), calls=%async_computation.3 | async-start | bytes 131072 | tf_op jit(solution)/shard_map/hidden_of_all_groups/all_to_all | solution.py:422
  123.4 13.6 %all-gather.3 = bf16[1024,384]{1,0:T(8,128)(2,1)S(1)} all-gather(bf16[128,384]{1,0:T(8,128)(2,1)S(1)} %collective-permute-done.1.refs_1_), channel_id=5, replica_groups=mesh['dh'=2,'dl'=4,'y'=8,'zh'=2,'x'=4,'c'=2] {'x','c'}, dimensions={0}, use_global_device_ids=true | all-gather | bytes 884736 | tf_op jit(solution)/shard_map/d_pre_of_two_groups/all_gather | solution.py:456
  137.1 1.8 d_pre_of_two_groups.1
  138.9 4.8 %all-to-all-start.1 = ((bf16[4,96,1536]{2,1,0:T(8,128)(2,1)}), bf16[4,96,1536]{2,1,0:T(8,128)(2,1)S(1)}, u32[]{:S(2)}, u32[]{:S(2)}) async-start(bf16[4,96,1536]{2,1,0:T(8,128)(2,1)} %bitcast.26), calls=%async_computation.1 | async-start | bytes 2359296 | tf_op jit(solution)/shard_map/d_pre_of_two_groups/all_to_all | solution.py:422
  143.7 13.4 %all-gather.4 = bf16[64,32,128]{2,1,0:T(8,128)(2,1)S(1)} all-gather(bf16[8,32,128]{2,1,0:T(8,128)(2,1)S(1)} %all-to-all-done.3), channel_id=6, replica_groups=mesh['dh'=2,'dl'=4,'y'=8,'zh'=2,'x'=4,'c'=2] {'x','c'}, dimensions={0}, use_global_device_ids=true | all-gather | bytes 589824 | tf_op jit(solution)/shard_map/hidden_of_all_groups/all_gather | solution.py:474
  157.1 13.7 %all-gather.12.cloned.1.call-done = bf16[64,32,768]{2,1,0:T(8,128)(2,1)} async-done(((bf16[8,32,768]{2,1,0:T(8,128)(2,1)}), bf16[64,32,768]{2,1,0:T(8,128)(2,1)}) %all-gather.12.cloned.1.call-update) | async-done | bytes 3145744 | tf_op jit(solution)/shard_map/cotangent_of_all_groups/all_gather | solution.py:468
  170.8 3.0 %hidden_of_all_groups.3 = (bf16[128,768]{1,0:T(8,128)(2,1)}, f32[8,128]{1,0:T(8,128)}) custom-call(bf16[8,8,32,128]{3,2,1,0:T(8,128)(2,1)S(1)} %bitcast.22, bf16[8,8,32,768]{3,2,1,0:T(8,128)(2,1)} %bitcast.27), custom_call_target="tpu_custom_call" | custom-call | tf_op jit(solution)/shard_map/hidden_of_all_groups/pallas_call | solution.py:335
  173.8 0.9 grad_in_sum.1
  (9 shorter events, 0.0 us)
Async XLA Ops:
  7.2 110.2 %all-gather.10.cloned.1.call-start = ((), (), s32[]{:S(2)}) async-start(), calls=%async_computation.4 | async-start | bytes 1327104 | tf_op jit(solution)/shard_map/cotangent_of_all_groups/all_gather | solution.py:466
  56.0 35.6 %all-to-all-start = ((bf16[8,128,768]{2,1,0:T(8,128)(2,1)}), bf16[8,128,768]{2,1,0:T(8,128)(2,1)S(1)}, u32[]{:S(2)}, u32[]{:S(2)}) async-start(bf16[8,128,768]{2,1,0:T(8,128)(2,1)} %bitcast.28), calls=%async_computation | async-start | bytes 3145728 | tf_op jit(solution)/shard_map/units/all_to_all | solution.py:422
  70.9 46.4 %collective-permute-start = (bf16[384,256]{1,0:T(8,128)(2,1)S(1)}, bf16[384,256]{1,0:T(8,128)(2,1)S(1)}, u32[]{:S(2)}, u32[]{:S(2)}) collective-permute-start(bf16[384,256]{1,0:T(8,128)(2,1)S(1)} %get-tuple-element.12), channel_id=1, source_target_pairs={{0,512},{512,0},{1,513},{513,1},{2,514},{514,2},{3,515},{515,3},{4... | collective-permute-start | bytes 589832 | tf_op jit(solution)/shard_map/y_of_two_groups/ppermute | solution.py:416
  93.9 22.8 %all-to-all-start.2 = ((bf16[8,32,384]{2,1,0:T(8,128)(2,1)}), bf16[8,32,384]{2,1,0:T(8,128)(2,1)S(1)}, u32[]{:S(2)}, u32[]{:S(2)}) async-start(bf16[8,32,384]{2,1,0:T(8,128)(2,1)} %bitcast.8), calls=%async_computation.2 | async-start | bytes 393216 | tf_op jit(solution)/shard_map/hidden_of_all_groups/all_to_all | solution.py:422
  97.9 72.9 %all-gather.12.cloned.1.call-start = ((), (), s32[]{:S(2)}) async-start(), calls=%async_computation.5 | async-start | bytes 3538944 | tf_op jit(solution)/shard_map/cotangent_of_all_groups/all_gather | solution.py:468
  97.9 19.4 %collective-permute-start.1 = (bf16[128,384]{1,0:T(8,128)(2,1)S(1)}, bf16[128,384]{1,0:T(8,128)(2,1)S(1)}, u32[]{:S(2)}, u32[]{:S(2)}) collective-permute-start(bf16[128,384]{1,0:T(8,128)(2,1)S(1)} %get-tuple-element.14), channel_id=1, source_target_pairs={{0,512},{512,0},{1,513},{513,1},{2,514},{514,2},{3,515},{515,3},{4... | collective-permute-start | bytes 294920 | tf_op jit(solution)/shard_map/d_pre_of_two_groups/ppermute | solution.py:416
  119.2 19.7 %all-to-all-start.3 = ((bf16[8,32,128]{2,1,0:T(8,128)(2,1)}), bf16[8,32,128]{2,1,0:T(8,128)(2,1)S(1)}, u32[]{:S(2)}, u32[]{:S(2)}) async-start(bf16[8,32,128]{2,1,0:T(8,128)(2,1)} %hidden_of_all_groups.2.refs_0_), calls=%async_computation.3 | async-start | bytes 131072 | tf_op jit(solution)/shard_map/hidden_of_all_groups/all_to_all | solution.py:422
  138.9 34.9 %all-to-all-start.1 = ((bf16[4,96,1536]{2,1,0:T(8,128)(2,1)}), bf16[4,96,1536]{2,1,0:T(8,128)(2,1)S(1)}, u32[]{:S(2)}, u32[]{:S(2)}) async-start(bf16[4,96,1536]{2,1,0:T(8,128)(2,1)} %bitcast.26), calls=%async_computation.1 | async-start | bytes 2359296 | tf_op jit(solution)/shard_map/d_pre_of_two_groups/all_to_all | solution.py:422
Sparse Core Ops, SparseCore 0:
  29.6 70.1 all-gather.9
  119.3 51.4 all-gather.11
where the time goes:
time: 182 us
  blocking collectives  83.8 us (46%)
  starting transfers between devices  36.7 us (20%)
  waiting for transfers between devices  30 us (16%)
  Pallas kernels  16.9 us (9%)
  between operations  14.1 us (8%)
    all_to_all x4, starting transfers between devices, send(): return lax.all_to_all(flat, axis, 0, 0, tiled=True).reshape(shape)  27.9 us
    all_gather x1, blocking collectives, shards(): gathered = lax.all_gather(rows, 'y', axis=0, tiled=False)  22.1 us
    all_gather x1, blocking collectives, shards(): rows = lax.all_gather(mine, 'zh', axis=0, tiled=False)  20.3 us
    all_to_all x4, waiting for transfers between devices, send(): return lax.all_to_all(flat, axis, 0, 0, tiled=True).reshape(shape)  16.3 us
    all_gather x1, blocking collectives, shards(): own = lax.all_gather(d_pre, MY, axis=0, tiled=False)  14.4 us
    all_gather x1, waiting for transfers between devices, shards(): cot_all = lax.all_gather(cot_rows, 'y', axis=0, tiled=False)  13.7 us
    all_gather x1, blocking collectives, shards(): other = lax.all_gather(d_pre_other, MY, axis=0, tiled=False)  13.6 us
    all_gather x1, blocking collectives, shards(): owned = lax.all_gather(send(owned, DP), MY, axis=0, tiled=False)  13.4 us
  transfers between devices with their start and end apart: 8, of which 2 were waited for; matrix products, arithmetic and copies ran while one was open for 0% of the time, Pallas kernels for 7%

commit v1 on v0

--- a/solution.py
+++ b/solution.py
@@ -17,7 +17,8 @@
 VMEM_LIMIT = 48 * 2**20
 
 DP = ("dh", "dl")
-MX = ("y", "zh")
+Y = ("yh", "yl")
+MX = Y + ("zh",)
 MY = ("x", "c")
 
 F32 = jnp.float32
@@ -437,7 +438,9 @@
         mine = norm_rows(place, tokens, cotangent)
         rows = lax.all_gather(mine, "zh", axis=0, tiled=False)
         longer = longer_rows(rows)
-        gathered = lax.all_gather(rows, "y", axis=0, tiled=False)
+        near = lax.all_gather(rows, "yl", axis=0, tiled=False)
+        gathered = lax.all_gather(near, "yh", axis=0, tiled=False)
+        gathered = gathered.reshape((-1,) + rows.shape)
 
     with jax.named_scope("units"):
         partial, flag = products(gathered, w_in, w_out)
@@ -458,14 +461,14 @@
         grad_in = send(grad_in.reshape(4, dblock // 8, grad_in.shape[1]), "dl")
 
     with jax.named_scope("hidden_of_all_groups"):
-        pieces = send(hidden.reshape(parts, block, UNITS), MY)
-        owned = by_owner(place, pieces.reshape(kinds + (block, UNITS)), own)
+        blocks = send(hidden.reshape(parts, block, UNITS), MY)
+        owned = by_owner(place, blocks.reshape(kinds + (block, UNITS)), own)
 
     with jax.named_scope("cotangent_of_all_groups"):
         count = rows.shape[0] * rows.shape[2]
         cot_rows = lax.all_gather(longer, DP, axis=0, tiled=False)
-        cot_rows = cotangent_rows(cot_rows, count, (owned, d_pre_other, y_other))
-        cot_all = lax.all_gather(cot_rows, "y", axis=0, tiled=False)
+        cot_rows = cotangent_rows(cot_rows, count, (blocks, own, d_pre_other, y_other))
+        cot_all = lax.all_gather(cot_rows, Y, axis=0, tiled=False)
         held = cot_all.shape[0]
         cot_all = cot_all.reshape(held, groups, lines // held, block, dblock)
         cot_all = cot_all.swapaxes(1, 2).reshape(lines, groups, block, dblock)
@@ -483,7 +486,8 @@
 def solution(mesh):
     sizes = dict(mesh.shape)
     lines = sizes["mx"] // 2
-    cut = (2, sizes["dp"] // 2, lines, 2, sizes["my"] // 2, 2)
+    near = 2 if lines % 2 == 0 else 1
+    cut = (2, sizes["dp"] // 2, lines // near, near, 2, sizes["my"] // 2, 2)
     fine = Mesh(mesh.devices.reshape(cut), DP + MX + MY)
     return jax.shard_map(
         shards,

time: 182 us -> 180 us (0.989)
  blocking collectives: 83.8 us -> 87.1 us
  starting transfers between devices: 36.7 us -> 33.9 us
  waiting for transfers between devices: 30 us -> 27.4 us
    all_to_all x4, starting transfers between devices: 27.9 us -> 23.8 us  [send(): return lax.all_to_all(flat, axis, 0, 0, tiled=True).reshape(shape)]
    all_gather x1, waiting for transfers between devices: 13.7 us -> 10.7 us  [shards(): cot_all = lax.all_gather(cot_rows, Y, axis=0, tiled=False)]
    all_gather x1 -> x2, blocking collectives: 22.1 us -> 24.9 us  [the longest x1 20.4 us: shards(): gathered = lax.all_gather(near, 'yh', axis=0, tiled=False)]
  transfers between devices with their start and end apart: 8 -> 8, of which waited for: 2 -> 3; matrix products, arithmetic and copies ran while one was open for 0% -> 0% of each run, Pallas kernels for 7% -> 7%
where the time goes in v1:
time: 180 us; the launch traced here: 179 us
  blocking collectives  87.1 us (48%)
  starting transfers between devices  33.9 us (19%)
  waiting for transfers between devices  27.4 us (15%)
  Pallas kernels  16.9 us (9%)
  between operations  14.1 us (8%)
    all_to_all x4, starting transfers between devices, send(): return lax.all_to_all(flat, axis, 0, 0, tiled=True).reshape(shape)  23.8 us
    all_gather x1, blocking collectives, shards(): gathered = lax.all_gather(near, 'yh', axis=0, tiled=False)  20.4 us
    all_gather x1, blocking collectives, shards(): rows = lax.all_gather(mine, 'zh', axis=0, tiled=False)  20.3 us
    all_to_all x4, waiting for transfers between devices, send(): return lax.all_to_all(flat, axis, 0, 0, tiled=True).reshape(shape)  16.6 us
    all_gather x1, blocking collectives, shards(): own = lax.all_gather(d_pre, MY, axis=0, tiled=False)  14.9 us
    all_gather x1, blocking collectives, shards(): other = lax.all_gather(d_pre_other, MY, axis=0, tiled=False)  13.6 us
    all_gather x1, blocking collectives, shards(): owned = lax.all_gather(send(owned, DP), MY, axis=0, tiled=False)  13.4 us
    all_gather x1, waiting for transfers between devices, shards(): cot_all = lax.all_gather(cot_rows, Y, axis=0, tiled=False)  10.7 us
  transfers between devices with their start and end apart: 8, of which 3 were waited for; matrix products, arithmetic and copies ran while one was open for 0% of the time, Pallas kernels for 7%

profile of v1, /device:TPU:1, one launch (start us, length us, event | category | flops | bytes accessed | tf_op | source)
XLA Modules:
  0.0 179.4 jit_solution(10104147125815351853)
XLA Ops:
  7.2 1.3 token_rows.2
  8.5 20.3 %all-gather = bf16[4,16,768]{2,1,0:T(8,128)(2,1)S(1)} all-gather(bf16[2,16,768]{2,1,0:T(8,128)(2,1)S(1)} %token_rows.2), channel_id=2, replica_groups=mesh['dh'=2,'dl'=4,'yh'=4,'yl'=2,'zh'=2,'x'=4,'c'=2] {'zh'}, dimensions={0}, use_global_device_ids=true | all-gather | bytes 147456 | tf_op jit(solution)/shard_map/token_rows/all_gather | solution.py:439
  28.8 0.7 token_rows.3
  29.5 4.4 %all-gather.1 = bf16[4,2,16,768]{3,2,1,0:T(8,128)(2,1)S(1)} all-gather(bf16[2,2,16,768]{3,2,1,0:T(8,128)(2,1)S(1)} %bitcast.22), channel_id=3, replica_groups=mesh['dh'=2,'dl'=4,'yh'=4,'yl'=2,'zh'=2,'x'=4,'c'=2] {'yl'}, dimensions={0}, use_global_device_ids=true | all-gather | bytes 294912 | tf_op jit(solution)/shard_map/token_rows/all_gather | solution.py:441
  33.9 20.4 %all-gather.2.y_ref.cot_ref.keep_in.give_in = bf16[8,2,2,16,768]{4,3,2,1,0:T(8,128)(2,1)S(1)} all-gather(bf16[2,2,2,16,768]{4,3,2,1,0:T(8,128)(2,1)S(1)} %bitcast.27), channel_id=4, replica_groups=mesh['dh'=2,'dl'=4,'yh'=4,'yl'=2,'zh'=2,'x'=4,'c'=2] {'yh'}, dimensions={0}, use_global_device_ids=true | all-gather | bytes 983040 | tf_op jit(solution)/shard_map/token_rows/all_gather | solution.py:442
  54.4 4.4 %units.2 = (bf16[2,2,2,128,768]{4,3,2,1,0:T(8,128)(2,1)}, f32[8,128]{1,0:T(8,128)}) custom-call(bf16[8,2,2,16,768]{4,3,2,1,0:T(8,128)(2,1)S(1)} %all-gather.2.y_ref.cot_ref.keep_in.give_in, bf16[8,2,2,16,768]{4,3,2,1,0:T(8,128)(2,1)S(1)} %all-gather.2.y_ref.cot_ref.keep_in.give_in, bf16[768,1536]{1,0:T(8,128)(2,1)} %w_ref.1, bf16[1024,768]{1,0:T(8,128)(2,1)} %vc.1, ...), custom_call_target="tpu_custom_call" | custom-call | tf_op jit(solution)/shard_map/units/pallas_call | solution.py:134
  58.8 10.3 %all-to-all-start = ((bf16[8,128,768]{2,1,0:T(8,128)(2,1)}), bf16[8,128,768]{2,1,0:T(8,128)(2,1)S(1)}, u32[]{:S(2)}, u32[]{:S(2)}) async-start(bf16[8,128,768]{2,1,0:T(8,128)(2,1)} %bitcast.25), calls=%async_computation | async-start | bytes 3145728 | tf_op jit(solution)/shard_map/units/all_to_all | solution.py:423
  69.2 5.1 %collective-permute-start = (bf16[384,256]{1,0:T(8,128)(2,1)S(1)}, bf16[384,256]{1,0:T(8,128)(2,1)S(1)}, u32[]{:S(2)}, u32[]{:S(2)}) collective-permute-start(bf16[384,256]{1,0:T(8,128)(2,1)S(1)} %get-tuple-element.12), channel_id=1, source_target_pairs={{0,512},{512,0},{1,513},{513,1},{2,514},{514,2},{3,515},{515,3},{4... | collective-permute-start | bytes 589832 | tf_op jit(solution)/shard_map/y_of_two_groups/ppermute | solution.py:417
  74.3 15.6 %all-to-all-done.terms_ref = bf16[8,128,768]{2,1,0:T(8,128)(2,1)S(1)} async-done(((bf16[8,128,768]{2,1,0:T(8,128)(2,1)}), bf16[8,128,768]{2,1,0:T(8,128)(2,1)S(1)}, u32[]{:S(2)}, u32[]{:S(2)}) %all-to-all-start) | async-done | bytes 1572896 | tf_op jit(solution)/shard_map/units/all_to_all | solution.py:423
  89.9 2.3 %units.3 = (bf16[2,128,384]{2,1,0:T(8,128)(2,1)}, bf16[128,384]{1,0:T(8,128)(2,1)S(1)}) custom-call(s32[1]{0:T(128)} %bitcast.1.place_ref, bf16[8,128,768]{2,1,0:T(8,128)(2,1)S(1)} %all-to-all-done.terms_ref, bf16[384,256]{1,0:T(8,128)(2,1)S(1)} %get-tuple-element.11.earlier_ref.y_own_ref), custom_call_target="tpu_custom_call" | custom-call | tf_op jit(solution)/shard_map/units/pallas_call | solution.py:214
  92.2 5.0 %collective-permute-start.1 = (bf16[128,384]{1,0:T(8,128)(2,1)S(1)}, bf16[128,384]{1,0:T(8,128)(2,1)S(1)}, u32[]{:S(2)}, u32[]{:S(2)}) collective-permute-start(bf16[128,384]{1,0:T(8,128)(2,1)S(1)} %get-tuple-element.14), channel_id=1, source_target_pairs={{0,512},{512,0},{1,513},{513,1},{2,514},{514,2},{3,515},{515,3},{4... | collective-permute-start | bytes 294920 | tf_op jit(solution)/shard_map/d_pre_of_two_groups/ppermute | solution.py:417
  97.1 4.5 %all-to-all-start.2 = ((bf16[8,32,384]{2,1,0:T(8,128)(2,1)}), bf16[8,32,384]{2,1,0:T(8,128)(2,1)S(1)}, u32[]{:S(2)}, u32[]{:S(2)}) async-start(bf16[8,32,384]{2,1,0:T(8,128)(2,1)} %bitcast.8), calls=%async_computation.2 | async-start | bytes 393216 | tf_op jit(solution)/shard_map/hidden_of_all_groups/all_to_all | solution.py:423
  101.6 14.9 %all-gather.3 = bf16[1024,384]{1,0:T(8,128)(2,1)S(1)} all-gather(bf16[128,384]{1,0:T(8,128)(2,1)S(1)} %get-tuple-element.14), channel_id=5, replica_groups=mesh['dh'=2,'dl'=4,'yh'=4,'yl'=2,'zh'=2,'x'=4,'c'=2] {'x','c'}, dimensions={0}, use_global_device_ids=true | all-gather | bytes 884736 | tf_op jit(solution)/shard_map/d_pre_of_two_groups/all_gather | solution.py:458
  116.5 1.8 cotangent_of_all_groups.1
  118.3 0.7 hidden_of_all_groups.2
  119.0 4.2 %all-to-all-start.3 = ((bf16[8,32,128]{2,1,0:T(8,128)(2,1)}), bf16[8,32,128]{2,1,0:T(8,128)(2,1)S(1)}, u32[]{:S(2)}, u32[]{:S(2)}) async-start(bf16[8,32,128]{2,1,0:T(8,128)(2,1)} %hidden_of_all_groups.2), calls=%async_computation.3 | async-start | bytes 131072 | tf_op jit(solution)/shard_map/hidden_of_all_groups/all_to_all | solution.py:423
  123.3 13.6 %all-gather.4 = bf16[1024,384]{1,0:T(8,128)(2,1)S(1)} all-gather(bf16[128,384]{1,0:T(8,128)(2,1)S(1)} %collective-permute-done.1.refs_2_), channel_id=6, replica_groups=mesh['dh'=2,'dl'=4,'yh'=4,'yl'=2,'zh'=2,'x'=4,'c'=2] {'x','c'}, dimensions={0}, use_global_device_ids=true | all-gather | bytes 884736 | tf_op jit(solution)/shard_map/d_pre_of_two_groups/all_gather | solution.py:459
  136.9 1.8 d_pre_of_two_groups.1
  138.7 4.8 %all-to-all-start.1 = ((bf16[4,96,1536]{2,1,0:T(8,128)(2,1)}), bf16[4,96,1536]{2,1,0:T(8,128)(2,1)S(1)}, u32[]{:S(2)}, u32[]{:S(2)}) async-start(bf16[4,96,1536]{2,1,0:T(8,128)(2,1)} %bitcast.23), calls=%async_computation.1 | async-start | bytes 2359296 | tf_op jit(solution)/shard_map/d_pre_of_two_groups/all_to_all | solution.py:423
  143.5 13.4 %all-gather.5 = bf16[64,32,128]{2,1,0:T(8,128)(2,1)S(1)} all-gather(bf16[8,32,128]{2,1,0:T(8,128)(2,1)S(1)} %all-to-all-done.3), channel_id=7, replica_groups=mesh['dh'=2,'dl'=4,'yh'=4,'yl'=2,'zh'=2,'x'=4,'c'=2] {'x','c'}, dimensions={0}, use_global_device_ids=true | all-gather | bytes 589824 | tf_op jit(solution)/shard_map/hidden_of_all_groups/all_gather | solution.py:477
  156.9 10.7 %all-gather.13.cloned.1.call-done = bf16[64,32,768]{2,1,0:T(8,128)(2,1)} async-done(((bf16[8,32,768]{2,1,0:T(8,128)(2,1)}), bf16[64,32,768]{2,1,0:T(8,128)(2,1)}) %all-gather.13.cloned.1.call-update) | async-done | bytes 3145744 | tf_op jit(solution)/shard_map/cotangent_of_all_groups/all_gather | solution.py:471
  167.6 3.0 %hidden_of_all_groups.3 = (bf16[128,768]{1,0:T(8,128)(2,1)}, f32[8,128]{1,0:T(8,128)}) custom-call(bf16[8,8,32,128]{3,2,1,0:T(8,128)(2,1)S(1)} %bitcast.19, bf16[8,8,32,768]{3,2,1,0:T(8,128)(2,1)} %bitcast.24), custom_call_target="tpu_custom_call" | custom-call | tf_op jit(solution)/shard_map/hidden_of_all_groups/pallas_call | solution.py:336
  170.6 1.1 all-to-all-done.1.parts_ref
  171.7 0.9 grad_in_sum.1
  (10 shorter events, 0.3 us)
Async XLA Ops:
  7.2 109.4 %all-gather.11.cloned.1.call-start = ((), (), s32[]{:S(2)}) async-start(), calls=%async_computation.4 | async-start | bytes 1327104 | tf_op jit(solution)/shard_map/cotangent_of_all_groups/all_gather | solution.py:469
  58.8 31.1 %all-to-all-start = ((bf16[8,128,768]{2,1,0:T(8,128)(2,1)}), bf16[8,128,768]{2,1,0:T(8,128)(2,1)S(1)}, u32[]{:S(2)}, u32[]{:S(2)}) async-start(bf16[8,128,768]{2,1,0:T(8,128)(2,1)} %bitcast.25), calls=%async_computation | async-start | bytes 3145728 | tf_op jit(solution)/shard_map/units/all_to_all | solution.py:423
  69.2 47.3 %collective-permute-start = (bf16[384,256]{1,0:T(8,128)(2,1)S(1)}, bf16[384,256]{1,0:T(8,128)(2,1)S(1)}, u32[]{:S(2)}, u32[]{:S(2)}) collective-permute-start(bf16[384,256]{1,0:T(8,128)(2,1)S(1)} %get-tuple-element.12), channel_id=1, source_target_pairs={{0,512},{512,0},{1,513},{513,1},{2,514},{514,2},{3,515},{515,3},{4... | collective-permute-start | bytes 589832 | tf_op jit(solution)/shard_map/y_of_two_groups/ppermute | solution.py:417
  92.2 24.4 %collective-permute-start.1 = (bf16[128,384]{1,0:T(8,128)(2,1)S(1)}, bf16[128,384]{1,0:T(8,128)(2,1)S(1)}, u32[]{:S(2)}, u32[]{:S(2)}) collective-permute-start(bf16[128,384]{1,0:T(8,128)(2,1)S(1)} %get-tuple-element.14), channel_id=1, source_target_pairs={{0,512},{512,0},{1,513},{513,1},{2,514},{514,2},{3,515},{515,3},{4... | collective-permute-start | bytes 294920 | tf_op jit(solution)/shard_map/d_pre_of_two_groups/ppermute | solution.py:417
  97.1 19.4 %all-to-all-start.2 = ((bf16[8,32,384]{2,1,0:T(8,128)(2,1)}), bf16[8,32,384]{2,1,0:T(8,128)(2,1)S(1)}, u32[]{:S(2)}, u32[]{:S(2)}) async-start(bf16[8,32,384]{2,1,0:T(8,128)(2,1)} %bitcast.8), calls=%async_computation.2 | async-start | bytes 393216 | tf_op jit(solution)/shard_map/hidden_of_all_groups/all_to_all | solution.py:423
  101.6 66.0 %all-gather.13.cloned.1.call-start = ((), (), s32[]{:S(2)}) async-start(), calls=%async_computation.5 | async-start | bytes 3538944 | tf_op jit(solution)/shard_map/cotangent_of_all_groups/all_gather | solution.py:471
  119.0 19.7 %all-to-all-start.3 = ((bf16[8,32,128]{2,1,0:T(8,128)(2,1)}), bf16[8,32,128]{2,1,0:T(8,128)(2,1)S(1)}, u32[]{:S(2)}, u32[]{:S(2)}) async-start(bf16[8,32,128]{2,1,0:T(8,128)(2,1)} %hidden_of_all_groups.2), calls=%async_computation.3 | async-start | bytes 131072 | tf_op jit(solution)/shard_map/hidden_of_all_groups/all_to_all | solution.py:423
  138.7 33.0 %all-to-all-start.1 = ((bf16[4,96,1536]{2,1,0:T(8,128)(2,1)}), bf16[4,96,1536]{2,1,0:T(8,128)(2,1)S(1)}, u32[]{:S(2)}, u32[]{:S(2)}) async-start(bf16[4,96,1536]{2,1,0:T(8,128)(2,1)} %bitcast.23), calls=%async_computation.1 | async-start | bytes 2359296 | tf_op jit(solution)/shard_map/d_pre_of_two_groups/all_to_all | solution.py:423
Sparse Core Ops, SparseCore 0:
  29.6 69.2 all-gather.10
  118.5 49.0 all-gather.12

commit v2 on v1

--- a/solution.py
+++ b/solution.py
@@ -234,18 +234,24 @@
     )(place, terms, earlier)
 
 
-def by_owner_kernel(place_ref, pieces_ref, earlier_ref, out_ref):
+def by_owner_kernel(place_ref, pieces_ref, rows_ref, *refs):
+    out_ref, cot_ref = refs[-2:]
     for s in range(2):
         out_ref[s] = pieces_ref[0, 0, s, :, :HEAD]
         for a in range(3):
             out_ref[2 + 3 * s + a] = pieces_ref[1, 0, s, :, a * HEAD : (a + 1) * HEAD]
-
-
-def by_owner(place, pieces, earlier):
+    cot_ref[...] = rows_ref[...]
+
+
+def by_owner(place, pieces, gathered, count, earlier):
     rows = pieces.shape[-2]
+    groups, _, dblock = gathered.shape
     return pl.pallas_call(
         by_owner_kernel,
-        out_shape=jax.ShapeDtypeStruct((8, rows, HEAD), BF16),
+        out_shape=(
+            pltpu.HBM((8, rows, HEAD), BF16),
+            pltpu.HBM((groups, count, dblock), BF16),
+        ),
         grid_spec=pltpu.PrefetchScalarGridSpec(
             num_scalar_prefetch=1,
             grid=(1,),
@@ -253,13 +259,17 @@
                 pl.BlockSpec(
                     (2, 1, 2, rows, UNITS), lambda s, place: (0, place[0] // 4, 0, 0, 0)
                 ),
-                pl.BlockSpec(memory_space=pl.ANY),
+                pl.BlockSpec((groups, count, dblock), lambda s, place: (0, 0, 0)),
+            ]
+            + [pl.BlockSpec(memory_space=pl.ANY)] * len(earlier),
+            out_specs=[
+                pl.BlockSpec((8, rows, HEAD), lambda s, place: (0, 0, 0)),
+                pl.BlockSpec((groups, count, dblock), lambda s, place: (0, 0, 0)),
             ],
-            out_specs=pl.BlockSpec((8, rows, HEAD), lambda s, place: (0, 0, 0)),
-        ),
-        compiler_params=params(),
-        interpret=INTERPRET,
-    )(place, pieces, earlier)
+        ),
+        compiler_params=params(),
+        interpret=INTERPRET,
+    )(place, pieces, stay(gathered), *earlier)
 
 
 def halves_kernel(side_ref, keep_in, give_in, earlier_ref, keep_ref, give_ref):
@@ -289,24 +299,6 @@
         compiler_params=params(),
         interpret=INTERPRET,
     )(side, gathered, gathered, stay(earlier))
-
-
-def cotangent_kernel(rows_ref, *refs):
-    refs[-1][...] = rows_ref[...]
-
-
-def cotangent_rows(gathered, count, earlier):
-    groups, _, dblock = gathered.shape
-    part = pl.BlockSpec((groups, count, dblock), lambda s: (0, 0, 0))
-    return pl.pallas_call(
-        cotangent_kernel,
-        out_shape=pltpu.HBM((groups, count, dblock), BF16),
-        grid=(1,),
-        in_specs=[part] + [pl.BlockSpec(memory_space=pl.ANY)] * len(earlier),
-        out_specs=part,
-        compiler_params=params(),
-        interpret=INTERPRET,
-    )(stay(gathered), *earlier)
 
 
 def grad_out_kernel(hidden_ref, cot_ref, out_ref, flag_ref, sum_ref):
@@ -462,12 +454,13 @@
 
     with jax.named_scope("hidden_of_all_groups"):
         blocks = send(hidden.reshape(parts, block, UNITS), MY)
-        owned = by_owner(place, blocks.reshape(kinds + (block, UNITS)), own)
+        blocks = blocks.reshape(kinds + (block, UNITS))
 
     with jax.named_scope("cotangent_of_all_groups"):
         count = rows.shape[0] * rows.shape[2]
         cot_rows = lax.all_gather(longer, DP, axis=0, tiled=False)
-        cot_rows = cotangent_rows(cot_rows, count, (blocks, own, d_pre_other, y_other))
+        ready = (own, d_pre_other, y_other)
+        owned, cot_rows = by_owner(place, blocks, cot_rows, count, ready)
         cot_all = lax.all_gather(cot_rows, Y, axis=0, tiled=False)
         held = cot_all.shape[0]
         cot_all = cot_all.reshape(held, groups, lines // held, block, dblock)

time: 180 us -> 179 us (level)
  no operation moved by 1% of the time
where the time goes in v2:
time: 179 us
  blocking collectives  87.1 us (49%)
  starting transfers between devices  33.9 us (19%)
  waiting for transfers between devices  27.4 us (15%)
  Pallas kernels  16.3 us (9%)
  between operations  14.1 us (8%)
    all_to_all x4, starting transfers between devices, send(): return lax.all_to_all(flat, axis, 0, 0, tiled=True).reshape(shape)  23.8 us
    all_gather x1, blocking collectives, shards(): gathered = lax.all_gather(near, 'yh', axis=0, tiled=False)  20.4 us
    all_gather x1, blocking collectives, shards(): rows = lax.all_gather(mine, 'zh', axis=0, tiled=False)  20.3 us
    all_to_all x4, waiting for transfers between devices, send(): return lax.all_to_all(flat, axis, 0, 0, tiled=True).reshape(shape)  16 us
    all_gather x1, blocking collectives, shards(): own = lax.all_gather(d_pre, MY, axis=0, tiled=False)  14.9 us
    all_gather x1, blocking collectives, shards(): other = lax.all_gather(d_pre_other, MY, axis=0, tiled=False)  13.6 us
    all_gather x1, blocking collectives, shards(): owned = lax.all_gather(send(owned, DP), MY, axis=0, tiled=False)  13.4 us
    all_gather x1, waiting for transfers between devices, shards(): cot_all = lax.all_gather(cot_rows, Y, axis=0, tiled=False)  11.4 us
  transfers between devices with their start and end apart: 8, of which 3 were waited for; matrix products, arithmetic and copies ran while one was open for 0% of the time, Pallas kernels for 7%

profile of v2, /device:TPU:1, one launch (start us, length us, event | category | flops | bytes accessed | tf_op | source)
XLA Modules:
  0.0 178.8 jit_solution(2842061366231086345)
XLA Ops:
  7.2 1.3 token_rows.2
  8.5 20.3 %all-gather = bf16[4,16,768]{2,1,0:T(8,128)(2,1)S(1)} all-gather(bf16[2,16,768]{2,1,0:T(8,128)(2,1)S(1)} %token_rows.2), channel_id=2, replica_groups=mesh['dh'=2,'dl'=4,'yh'=4,'yl'=2,'zh'=2,'x'=4,'c'=2] {'zh'}, dimensions={0}, use_global_device_ids=true | all-gather | bytes 147456 | tf_op jit(solution)/shard_map/token_rows/all_gather | solution.py:431
  28.8 0.7 token_rows.3
  29.5 4.4 %all-gather.1 = bf16[4,2,16,768]{3,2,1,0:T(8,128)(2,1)S(1)} all-gather(bf16[2,2,16,768]{3,2,1,0:T(8,128)(2,1)S(1)} %bitcast.20), channel_id=3, replica_groups=mesh['dh'=2,'dl'=4,'yh'=4,'yl'=2,'zh'=2,'x'=4,'c'=2] {'yl'}, dimensions={0}, use_global_device_ids=true | all-gather | bytes 294912 | tf_op jit(solution)/shard_map/token_rows/all_gather | solution.py:433
  33.9 20.4 %all-gather.2.y_ref.cot_ref.keep_in.give_in = bf16[8,2,2,16,768]{4,3,2,1,0:T(8,128)(2,1)S(1)} all-gather(bf16[2,2,2,16,768]{4,3,2,1,0:T(8,128)(2,1)S(1)} %bitcast.26), channel_id=4, replica_groups=mesh['dh'=2,'dl'=4,'yh'=4,'yl'=2,'zh'=2,'x'=4,'c'=2] {'yh'}, dimensions={0}, use_global_device_ids=true | all-gather | bytes 983040 | tf_op jit(solution)/shard_map/token_rows/all_gather | solution.py:434
  54.4 4.4 %units.2 = (bf16[2,2,2,128,768]{4,3,2,1,0:T(8,128)(2,1)}, f32[8,128]{1,0:T(8,128)}) custom-call(bf16[8,2,2,16,768]{4,3,2,1,0:T(8,128)(2,1)S(1)} %all-gather.2.y_ref.cot_ref.keep_in.give_in, bf16[8,2,2,16,768]{4,3,2,1,0:T(8,128)(2,1)S(1)} %all-gather.2.y_ref.cot_ref.keep_in.give_in, bf16[768,1536]{1,0:T(8,128)(2,1)} %w_ref.1, bf16[1024,768]{1,0:T(8,128)(2,1)} %vc.1, ...), custom_call_target="tpu_custom_call" | custom-call | tf_op jit(solution)/shard_map/units/pallas_call | solution.py:134
  58.8 10.3 %all-to-all-start = ((bf16[8,128,768]{2,1,0:T(8,128)(2,1)}), bf16[8,128,768]{2,1,0:T(8,128)(2,1)S(1)}, u32[]{:S(2)}, u32[]{:S(2)}) async-start(bf16[8,128,768]{2,1,0:T(8,128)(2,1)} %bitcast.24), calls=%async_computation | async-start | bytes 3145728 | tf_op jit(solution)/shard_map/units/all_to_all | solution.py:415
  69.1 0.2 y_of_two_groups.1
  69.2 5.1 %collective-permute-start = (bf16[384,256]{1,0:T(8,128)(2,1)S(1)}, bf16[384,256]{1,0:T(8,128)(2,1)S(1)}, u32[]{:S(2)}, u32[]{:S(2)}) collective-permute-start(bf16[384,256]{1,0:T(8,128)(2,1)S(1)} %get-tuple-element.14), channel_id=1, source_target_pairs={{0,512},{512,0},{1,513},{513,1},{2,514},{514,2},{3,515},{515,3},{4... | collective-permute-start | bytes 589832 | tf_op jit(solution)/shard_map/y_of_two_groups/ppermute | solution.py:409
  74.4 15.6 %all-to-all-done.terms_ref = bf16[8,128,768]{2,1,0:T(8,128)(2,1)S(1)} async-done(((bf16[8,128,768]{2,1,0:T(8,128)(2,1)}), bf16[8,128,768]{2,1,0:T(8,128)(2,1)S(1)}, u32[]{:S(2)}, u32[]{:S(2)}) %all-to-all-start) | async-done | bytes 1572896 | tf_op jit(solution)/shard_map/units/all_to_all | solution.py:415
  89.9 2.3 %units.3 = (bf16[2,128,384]{2,1,0:T(8,128)(2,1)}, bf16[128,384]{1,0:T(8,128)(2,1)S(1)}) custom-call(s32[1]{0:T(128)} %bitcast.1.place_ref, bf16[8,128,768]{2,1,0:T(8,128)(2,1)S(1)} %all-to-all-done.terms_ref, bf16[384,256]{1,0:T(8,128)(2,1)S(1)} %get-tuple-element.13.earlier_ref.y_own_ref), custom_call_target="tpu_custom_call" | custom-call | tf_op jit(solution)/shard_map/units/pallas_call | solution.py:214
  92.2 5.0 %collective-permute-start.1 = (bf16[128,384]{1,0:T(8,128)(2,1)S(1)}, bf16[128,384]{1,0:T(8,128)(2,1)S(1)}, u32[]{:S(2)}, u32[]{:S(2)}) collective-permute-start(bf16[128,384]{1,0:T(8,128)(2,1)S(1)} %get-tuple-element.16), channel_id=1, source_target_pairs={{0,512},{512,0},{1,513},{513,1},{2,514},{514,2},{3,515},{515,3},{4... | collective-permute-start | bytes 294920 | tf_op jit(solution)/shard_map/d_pre_of_two_groups/ppermute | solution.py:409
  97.2 4.5 %all-to-all-start.2 = ((bf16[8,32,384]{2,1,0:T(8,128)(2,1)}), bf16[8,32,384]{2,1,0:T(8,128)(2,1)S(1)}, u32[]{:S(2)}, u32[]{:S(2)}) async-start(bf16[8,32,384]{2,1,0:T(8,128)(2,1)} %bitcast.8), calls=%async_computation.2 | async-start | bytes 393216 | tf_op jit(solution)/shard_map/hidden_of_all_groups/all_to_all | solution.py:415
  101.6 14.9 %all-gather.3 = bf16[1024,384]{1,0:T(8,128)(2,1)S(1)} all-gather(bf16[128,384]{1,0:T(8,128)(2,1)S(1)} %get-tuple-element.16), channel_id=5, replica_groups=mesh['dh'=2,'dl'=4,'yh'=4,'yl'=2,'zh'=2,'x'=4,'c'=2] {'x','c'}, dimensions={0}, use_global_device_ids=true | all-gather | bytes 884736 | tf_op jit(solution)/shard_map/d_pre_of_two_groups/all_gather | solution.py:450
  116.6 1.8 %cotangent_of_all_groups.1 = (bf16[8,32,128]{2,1,0:T(8,128)(2,1)}, bf16[8,32,768]{2,1,0:T(8,128)(2,1)}) custom-call(s32[1]{0:T(128)} %bitcast.1.place_ref, bf16[2,2,2,32,384]{4,3,2,1,0:T(8,128)(2,1)S(1)} %bitcast.21, bf16[8,96,768]{2,1,0:T(8,128)(2,1)} %bitcast.25, bf16[8,128,384]{2,1,0:T(8,128)(2,1)S(1)} %bitcast.15, ...), custom_call_target="tpu_custom_call" | custom-call | tf_op jit(solution)/shard_map/cotangent_of_all_groups/pallas_call | solution.py:249
  118.4 4.3 %all-to-all-start.3 = ((bf16[8,32,128]{2,1,0:T(8,128)(2,1)}), bf16[8,32,128]{2,1,0:T(8,128)(2,1)S(1)}, u32[]{:S(2)}, u32[]{:S(2)}) async-start(bf16[8,32,128]{2,1,0:T(8,128)(2,1)} %get-tuple-element.18), calls=%async_computation.3 | async-start | bytes 131072 | tf_op jit(solution)/shard_map/hidden_of_all_groups/all_to_all | solution.py:415
  122.7 13.6 %all-gather.4 = bf16[1024,384]{1,0:T(8,128)(2,1)S(1)} all-gather(bf16[128,384]{1,0:T(8,128)(2,1)S(1)} %collective-permute-done.1.refs_1_), channel_id=6, replica_groups=mesh['dh'=2,'dl'=4,'yh'=4,'yl'=2,'zh'=2,'x'=4,'c'=2] {'x','c'}, dimensions={0}, use_global_device_ids=true | all-gather | bytes 884736 | tf_op jit(solution)/shard_map/d_pre_of_two_groups/all_gather | solution.py:451
  136.3 1.8 %d_pre_of_two_groups.1 = bf16[384,1536]{1,0:T(8,128)(2,1)} custom-call(bf16[384,256]{1,0:T(8,128)(2,1)S(1)} %get-tuple-element.13.earlier_ref.y_own_ref, bf16[384,256]{1,0:T(8,128)(2,1)S(1)} %collective-permute-done.y_other_ref.refs_2_, bf16[8,128,384]{2,1,0:T(8,128)(2,1)S(1)} %bitcast.16, bf16[8,128,384]{2,1,0:T(8,128)(2,1)S(1)} %bitcast.17), custom_call_target="tpu_custom_call" | custom-call | tf_op jit(solution)/shard_map/d_pre_of_two_groups/pallas_call | solution.py:374
  138.1 4.8 %all-to-all-start.1 = ((bf16[4,96,1536]{2,1,0:T(8,128)(2,1)}), bf16[4,96,1536]{2,1,0:T(8,128)(2,1)S(1)}, u32[]{:S(2)}, u32[]{:S(2)}) async-start(bf16[4,96,1536]{2,1,0:T(8,128)(2,1)} %bitcast.22), calls=%async_computation.1 | async-start | bytes 2359296 | tf_op jit(solution)/shard_map/d_pre_of_two_groups/all_to_all | solution.py:415
  142.9 13.4 %all-gather.6 = bf16[64,32,128]{2,1,0:T(8,128)(2,1)S(1)} all-gather(bf16[8,32,128]{2,1,0:T(8,128)(2,1)S(1)} %all-to-all-done.3), channel_id=8, replica_groups=mesh['dh'=2,'dl'=4,'yh'=4,'yl'=2,'zh'=2,'x'=4,'c'=2] {'x','c'}, dimensions={0}, use_global_device_ids=true | all-gather | bytes 589824 | tf_op jit(solution)/shard_map/hidden_of_all_groups/all_gather | solution.py:470
  156.3 11.4 %all-gather.13.cloned.1.call-done = bf16[64,32,768]{2,1,0:T(8,128)(2,1)} async-done(((bf16[8,32,768]{2,1,0:T(8,128)(2,1)}), bf16[64,32,768]{2,1,0:T(8,128)(2,1)}) %all-gather.13.cloned.1.call-update) | async-done | bytes 3145744 | tf_op jit(solution)/shard_map/cotangent_of_all_groups/all_gather | solution.py:464
  167.7 3.0 %hidden_of_all_groups.1 = (bf16[128,768]{1,0:T(8,128)(2,1)}, f32[8,128]{1,0:T(8,128)}) custom-call(bf16[8,8,32,128]{3,2,1,0:T(8,128)(2,1)S(1)} %bitcast.18, bf16[8,8,32,768]{3,2,1,0:T(8,128)(2,1)} %bitcast.23), custom_call_target="tpu_custom_call" | custom-call | tf_op jit(solution)/shard_map/hidden_of_all_groups/pallas_call | solution.py:328
  170.7 0.4 all-to-all-done.1.parts_ref
  171.1 0.9 grad_in_sum.1
  (9 shorter events, 0.1 us)
Async XLA Ops:
  7.2 109.4 %all-gather.11.cloned.1.call-start = ((), (), s32[]{:S(2)}) async-start(), calls=%async_computation.4 | async-start | bytes 1327104 | tf_op jit(solution)/shard_map/cotangent_of_all_groups/all_gather | solution.py:461
  58.8 31.1 %all-to-all-start = ((bf16[8,128,768]{2,1,0:T(8,128)(2,1)}), bf16[8,128,768]{2,1,0:T(8,128)(2,1)S(1)}, u32[]{:S(2)}, u32[]{:S(2)}) async-start(bf16[8,128,768]{2,1,0:T(8,128)(2,1)} %bitcast.24), calls=%async_computation | async-start | bytes 3145728 | tf_op jit(solution)/shard_map/units/all_to_all | solution.py:415
  69.2 47.3 %collective-permute-start = (bf16[384,256]{1,0:T(8,128)(2,1)S(1)}, bf16[384,256]{1,0:T(8,128)(2,1)S(1)}, u32[]{:S(2)}, u32[]{:S(2)}) collective-permute-start(bf16[384,256]{1,0:T(8,128)(2,1)S(1)} %get-tuple-element.14), channel_id=1, source_target_pairs={{0,512},{512,0},{1,513},{513,1},{2,514},{514,2},{3,515},{515,3},{4... | collective-permute-start | bytes 589832 | tf_op jit(solution)/shard_map/y_of_two_groups/ppermute | solution.py:409
  92.2 24.4 %collective-permute-start.1 = (bf16[128,384]{1,0:T(8,128)(2,1)S(1)}, bf16[128,384]{1,0:T(8,128)(2,1)S(1)}, u32[]{:S(2)}, u32[]{:S(2)}) collective-permute-start(bf16[128,384]{1,0:T(8,128)(2,1)S(1)} %get-tuple-element.16), channel_id=1, source_target_pairs={{0,512},{512,0},{1,513},{513,1},{2,514},{514,2},{3,515},{515,3},{4... | collective-permute-start | bytes 294920 | tf_op jit(solution)/shard_map/d_pre_of_two_groups/ppermute | solution.py:409
  97.2 19.4 %all-to-all-start.2 = ((bf16[8,32,384]{2,1,0:T(8,128)(2,1)}), bf16[8,32,384]{2,1,0:T(8,128)(2,1)S(1)}, u32[]{:S(2)}, u32[]{:S(2)}) async-start(bf16[8,32,384]{2,1,0:T(8,128)(2,1)} %bitcast.8), calls=%async_computation.2 | async-start | bytes 393216 | tf_op jit(solution)/shard_map/hidden_of_all_groups/all_to_all | solution.py:415
  101.6 66.1 %all-gather.13.cloned.1.call-start = ((), (), s32[]{:S(2)}) async-start(), calls=%async_computation.5 | async-start | bytes 3538944 | tf_op jit(solution)/shard_map/cotangent_of_all_groups/all_gather | solution.py:464
  118.4 19.7 %all-to-all-start.3 = ((bf16[8,32,128]{2,1,0:T(8,128)(2,1)}), bf16[8,32,128]{2,1,0:T(8,128)(2,1)S(1)}, u32[]{:S(2)}, u32[]{:S(2)}) async-start(bf16[8,32,128]{2,1,0:T(8,128)(2,1)} %get-tuple-element.18), calls=%async_computation.3 | async-start | bytes 131072 | tf_op jit(solution)/shard_map/hidden_of_all_groups/all_to_all | solution.py:415
  138.1 33.0 %all-to-all-start.1 = ((bf16[4,96,1536]{2,1,0:T(8,128)(2,1)}), bf16[4,96,1536]{2,1,0:T(8,128)(2,1)S(1)}, u32[]{:S(2)}, u32[]{:S(2)}) async-start(bf16[4,96,1536]{2,1,0:T(8,128)(2,1)} %bitcast.22), calls=%async_computation.1 | async-start | bytes 2359296 | tf_op jit(solution)/shard_map/d_pre_of_two_groups/all_to_all | solution.py:415
Sparse Core Ops, SparseCore 0:
  29.6 69.2 all-gather.10
  118.5 49.0 all-gather.12
